TPU v7x, 32 devices: a whole 2x2x4 slice. The times are simulated.
32 devices in a mesh: mol: 2 (over y), pair: 8 (over z, core), int: 2 (over x), rep: 1.
Axes of the slice: x: 2, y: 2, z: 4, core: 2. Of those that a mesh axis runs over, the one named last changes fastest.
Arguments:
- amplitudes: bfloat16 [64, 4, 32, 4096], P(('mol', 'pair'), None, ('int', 'rep')), parts along dimension 0, may hold values from -6 to 6
- amp_tiles: int32 [64, 4], P(('mol', 'pair')), parts along dimension 0, may hold values from 0 to 7, all different within a row; in each aligned block of 4 rows (0 to 3, 4 to 7, ...) at most 2 rows name the same one
- integrals: bfloat16 [16, 4096, 2, 4096], P(('mol', 'pair'), None, None, ('int', 'rep')), parts along dimension 0, may hold values from -0.09375 to 0.09375
- int_tiles: int32 [16, 2], P('mol'), parts along dimension 0, may hold values from 0 to 7, all different within a row
- occupied_energy: float32 [64, 32], P(('mol', 'pair')), parts along dimension 0, may hold values from -3 to -0.5
- virtual_energy: float32 [16, 4096], P('mol', ('int', 'rep')), parts along dimension 0, may hold values from 0.5 to 6
Outputs:
- amplitude_step: bfloat16 [64, 8, 32, 4096], P(('mol', 'pair'), None, None, ('int', 'rep')), parts along dimension 0
There are 2 independent parts, one for each index of `mol`. A program takes and returns all parts, laid end to end along the dimension named above; each array names one. Nothing has to cross between parts.
Inputs may be any that keep to these rules, and one draw needn't show every extreme that they name: `amp_tiles`: the 4 tiles of one row tile are distinct. Among the 4 row tiles of one pair index no virtual-pair tile is named more than 2 times, and in every draw some tile is named exactly 2 times by the row tiles of some pair index. `int_tiles`: the 2 tiles of one row are distinct, and every virtual-pair tile is named by some row.
All inputs are finite; a program needn't handle non-finite values.
Results may differ from a plain program's by a relative error of at most 0.0049.
Values may be sent and summed in bfloat16 or wider, within the bound.
A program may use at most 128 MiB of HBM per device.

v0:
```python
import jax
import jax.numpy as jnp
from jax import lax
from jax.sharding import PartitionSpec as P


def shards(amplitudes, amp_tiles, integrals, int_tiles, occupied_energy, virtual_energy):
    pair_count = lax.axis_size("pair")
    tile_total = int_tiles.shape[0]
    local_count = integrals.shape[0]
    row_tiles, slot_count, row_local, pair_width = amplitudes.shape
    couplings = integrals.shape[2]
    col_local = integrals.shape[3]
    entries = row_tiles * slot_count
    capacity = max(2, (entries + tile_total - 1) // tile_total)
    flat_tiles = amp_tiles.reshape(-1)
    tile_hits = (flat_tiles[:, None] == jnp.arange(tile_total, dtype=jnp.int32)[None, :]).astype(
        jnp.int32
    )
    slot_rank = jnp.sum(tile_hits * (jnp.cumsum(tile_hits, axis=0) - 1), axis=1)
    slot_index = flat_tiles * capacity + slot_rank
    buffer_slots = tile_total * capacity
    dispatch = (jnp.arange(buffer_slots, dtype=jnp.int32)[:, None] == slot_index[None, :]).astype(
        jnp.bfloat16
    )
    right_cols = integrals.reshape(local_count, pair_width, couplings * col_local)
    packed = jnp.dot(
        dispatch,
        amplitudes.reshape(entries, row_local * pair_width),
        preferred_element_type=jnp.float32,
    )
    packed = packed.astype(jnp.bfloat16).reshape(
        pair_count, local_count, capacity, row_local, pair_width
    )
    left_rows = lax.all_gather(
        lax.all_to_all(packed, "pair", split_axis=0, concat_axis=0, tiled=True),
        ("int", "rep"),
        axis=3,
        tiled=True,
    )[:, 0]
    shaped = left_rows.reshape(-1, pair_width)
    product = jnp.dot(shaped, right_cols[0], preferred_element_type=jnp.float32).astype(
        jnp.bfloat16
    )
    pieces = [product.reshape(left_rows.shape[:3] + (couplings, col_local))]
    stacked = jnp.stack(pieces, axis=1)
    returned = lax.all_to_all(stacked, "pair", split_axis=0, concat_axis=0, tiled=True)
    row_count = returned.shape[3]
    returned = returned.reshape(buffer_slots, row_count, couplings, col_local)
    targets = jnp.sum(tile_hits[:, :, None] * int_tiles[None, :, :], axis=1)
    row_owner = jnp.arange(entries, dtype=jnp.int32) // slot_count
    dest_rows = row_owner[:, None] * tile_total + targets
    landing = (
        jnp.arange(row_tiles * tile_total, dtype=jnp.int32)[:, None, None] == dest_rows[None, :, :]
    ).astype(jnp.bfloat16)
    combine = jnp.einsum(
        "qjk,sj->qsk", landing, dispatch, preferred_element_type=jnp.float32
    ).astype(jnp.bfloat16)
    residual = jnp.einsum("qsk,slkc->qlc", combine, returned, preferred_element_type=jnp.float32)
    residual = residual.reshape(row_tiles, tile_total, row_count, col_local)
    denominator = virtual_energy[None, :, None, :] - occupied_energy[:, None, :, None]
    return (residual / denominator).astype(jnp.bfloat16)


def solution(mesh):
    placed = (
        P(("mol", "pair"), None, ("int", "rep"), None),
        P(("mol", "pair"), None),
        P(("mol", "pair"), None, None, ("int", "rep")),
        P("mol", None),
        P(("mol", "pair"), None),
        P("mol", ("int", "rep")),
    )
    return jax.shard_map(
        shards,
        mesh=mesh,
        in_specs=placed,
        out_specs=P(("mol", "pair"), None, None, ("int", "rep")),
        check_vma=False,
    )
```

profile of v0, /device:TPU:0, one launch (start us, length us, event | category | flops | bytes accessed | tf_op | source)
XLA Modules:
  0.0 269.3 jit_solution(2620794862529324393)
XLA Ops:
  6.5 0.0 copy-start
  6.5 0.0 all-gather.2.cloned.1.call-start
  6.5 2.8 %copy.35 = bf16[2,8,16,4096]{3,1,2,0:T(8,128)(2,1)S(1)} copy(bf16[2,8,16,4096]{3,2,1,0:T(8,128)(2,1)} %bitcast.41) | data formatting | bytes 4194304
  9.3 0.0 copy-done
  9.3 0.1 eq.46
  9.4 0.1 fusion.6
  9.5 0.2 select_reduce_fusion
  9.7 0.7 convolution_convert_fusion
  10.4 1.2 copy.36
  11.6 55.3 %all_to_all.10 = bf16[8,1,2,16,4096]{4,3,2,1,0:T(8,128)(2,1)} all-to-all(bf16[8,1,2,16,4096]{4,3,2,1,0:T(8,128)(2,1)S(1)} %bitcast.40), channel_id=1, replica_groups=mesh['mol'=2,'pair'=8,'int'=2,'rep'=1] {'pair'}, dimensions={0} | all-to-all | bytes 4194304 | tf_op jit(solution)/shard_map/all_to_all | solution.py:36
  66.8 0.0 all-gather.2.cloned.1.call-update
  66.9 23.6 %copy.37 = bf16[512,8,2,2048]{3,1,2,0:T(8,128)(2,1)} copy(bf16[512,8,2,2048]{3,2,1,0:T(2,128)(2,1)} %bitcast.35) | data formatting | bytes 67108864
  90.5 32.2 %all-gather.2.cloned.1.call-done = bf16[8,1,2,32,4096]{4,3,2,1,0:T(8,128)(2,1)} async-done(((bf16[8,1,2,16,4096]{4,3,2,1,0:T(8,128)(2,1)}), bf16[8,1,2,32,4096]{4,3,2,1,0:T(8,128)(2,1)}) %all-gather.2.cloned.1.call-update) | async-done | bytes 4194320 | tf_op jit(solution)/shard_map/all_gather | solution.py:35
  122.7 23.6 %convolution_convert_fusion.1 = bf16[512,4096]{1,0:T(8,128)(2,1)} fusion(bf16[512,4096]{1,0:T(8,128)(2,1)} %bitcast.42, bf16[4096,4096]{1,0:T(8,128)(2,1)} %bitcast.36), kind=kOutput, calls=%fused_computation.3 | convolution fusion | flops 17181966336 | bytes 41943040 | tf_op jit(solution)/shard_map/dot_general | solution.py:42
  146.3 7.8 %stack_reshape.3 = bf16[8,1,2,32,2,2048]{5,4,3,2,0,1:T(2,128)(2,1)} reshape(bf16[512,4096]{1,0:T(8,128)(2,1)} %convolution_convert_fusion.1) | data formatting | bytes 8388608 | tf_op jit(solution)/shard_map/stack;reshape | solution.py:46
  154.1 0.0 copy-start.1
  154.1 0.0 copy-start.2
  154.1 0.0 copy-start.3
  154.1 4.9 %all-to-all-start.1 = ((bf16[8,1,2,32,2,2048]{5,4,3,2,1,0:T(2,128)(2,1)}), bf16[8,1,2,32,2,2048]{5,4,3,2,1,0:T(2,128)(2,1)}, u32[]{:S(2)}, u32[]{:S(2)}) async-start(bf16[8,1,2,32,2,2048]{5,4,3,2,1,0:T(2,128)(2,1)} %bitcast.37), calls=%async_computation.1 | async-start | bytes 8388608 | tf_op jit(solution)/shard_map/all_to_all | solution.py:47
  159.0 0.1 copy.23
  159.0 0.0 copy-done.1
  159.0 0.1 multiply_reduce_fusion
  159.1 0.2 convolution_convert_fusion.2
  159.3 0.1 copy.24
  159.4 93.5 %all-to-all-done.1 = bf16[8,1,2,32,2,2048]{5,4,3,2,1,0:T(2,128)(2,1)} async-done(((bf16[8,1,2,32,2,2048]{5,4,3,2,1,0:T(2,128)(2,1)}), bf16[8,1,2,32,2,2048]{5,4,3,2,1,0:T(2,128)(2,1)}, u32[]{:S(2)}, u32[]{:S(2)}) %all-to-all-start.1) | async-done | bytes 4194336 | tf_op jit(solution)/shard_map/all_to_all | solution.py:47
  252.9 0.0 copy-done.2
  252.9 0.0 copy-done.3
  252.9 5.2 %fusion = bf16[4,8,32,2048]{3,1,2,0:T(8,128)(2,1)S(1)} fusion(bf16[16,32,2,2048]{3,2,1,0:T(2,128)(2,1)} %bitcast.6, f32[4,32]{1,0:T(4,128)S(1)} %copy-done.3, f32[8,2048]{1,0:T(8,128)S(1)} %copy-done.2, bf16[32,2,16]{2,0,1:T(8,128)(2,1)S(1)} %copy.24), kind=kOutput, calls=%fused_computation.2 | convolution fusion | flops 140509184 | bytes 8456704 | tf_op jit(solution)/shard_map/qsk,slkc->qlc/dot_general | solution.py:59
  258.1 4.3 %copy.29 = bf16[4,8,32,2048]{3,2,1,0:T(8,128)(2,1)} copy(bf16[4,8,32,2048]{3,1,2,0:T(8,128)(2,1)S(1)} %fusion) | data formatting | bytes 8388608 | tf_op jit(solution)/shard_map/convert_element_type | solution.py:62
  (4 shorter events, 0.1 us)
Async XLA Ops:
  6.5 2.8 %copy-start = (s32[4,4]{1,0:T(4,128)S(1)}, s32[4,4]{1,0:T(4,128)}, u32[]{:S(2)}) copy-start(s32[4,4]{1,0:T(4,128)} %param.7) | copy-start | bytes 196
  6.5 116.2 %all-gather.2.cloned.1.call-start = ((), (), s32[]{:S(2)}) async-start(), calls=%async_computation.2 | async-start | bytes 6291456 | tf_op jit(solution)/shard_map/all_gather | solution.py:35
  154.1 4.9 %copy-start.1 = (s32[8,2]{0,1:T(2,128)S(1)}, s32[8,2]{0,1:T(2,128)}, u32[]{:S(2)}) copy-start(s32[8,2]{0,1:T(2,128)} %param.9) | copy-start | bytes 196
  154.1 98.9 %copy-start.2 = (f32[8,2048]{1,0:T(8,128)S(1)}, f32[8,2048]{1,0:T(8,128)}, u32[]{:S(2)}) copy-start(f32[8,2048]{1,0:T(8,128)} %param.11) | copy-start | bytes 196612
  154.1 98.9 %copy-start.3 = (f32[4,32]{1,0:T(4,128)S(1)}, f32[4,32]{1,0:T(4,128)}, u32[]{:S(2)}) copy-start(f32[4,32]{1,0:T(4,128)} %param.10) | copy-start | bytes 1540
  154.1 98.9 %all-to-all-start.1 = ((bf16[8,1,2,32,2,2048]{5,4,3,2,1,0:T(2,128)(2,1)}), bf16[8,1,2,32,2,2048]{5,4,3,2,1,0:T(2,128)(2,1)}, u32[]{:S(2)}, u32[]{:S(2)}) async-start(bf16[8,1,2,32,2,2048]{5,4,3,2,1,0:T(2,128)(2,1)} %bitcast.37), calls=%async_computation.1 | async-start | bytes 8388608 | tf_op jit(solution)/shard_map/all_to_all | solution.py:47
Sparse Core Ops, SparseCore 0:
  67.0 55.6 all-gather.1
where the time goes:
time: 270 us; the launch traced here: 269 us
  waiting for transfers between devices  126 us (47%)
  blocking collectives  55.3 us (20%)
  local copies, waits for them, and re-layouts  39.9 us (15%)
  matrix products  29.6 us (11%)
  between operations  13.4 us (5%)
  starting transfers between devices  4.86 us (2%)
    all_to_all x1, waiting for transfers between devices, shards(): lax.all_to_all(stacked, 'pair', split_axis=0, concat_axis=0, tiled=True)  93.5 us
    all_to_all x1, blocking collectives, shards(): lax.all_to_all(packed, 'pair', split_axis=0, concat_axis=0, tiled=True)  55.3 us
    all_gather x1, waiting for transfers between devices, shards(): lax.all_gather(lax.all_to_all(packed, 'pair', split_axis=0, concat_axis=0...  32.2 us
    unnamed x11, local copies, waits for them, and re-layouts  27.5 us
    dot_general x1, matrix products, shards(): jnp.dot(shaped, right_cols[0], preferred_element_type=jnp.float32)  23.6 us
    another operation x1, local copies, waits for them, and re-layouts, shards(): stacked = jnp.stack(pieces, axis=1)  7.82 us
  transfers between devices with their start and end apart: 2, of which 2 were waited for; matrix products, arithmetic and copies ran while one was open for 9% of the time, Pallas kernels for 0%

commit v1 on v0

v1 whole, which is shorter than its diff:
```python
import functools

import jax
import jax.numpy as jnp
from jax import lax
from jax.experimental import pallas as pl
from jax.experimental.pallas import tpu as pltpu
from jax.sharding import PartitionSpec as P

MESH = pl.DeviceIdType.MESH


def flip(index, mask, size):
    out, bit = 0, 1
    while bit < size:
        out = out + ((index // bit + mask // bit) % 2) * bit
        bit *= 2
    return out


def ladder(pairs, ints, reps, tile, packed, right, returned, left, slab, product,
           slab_sem, own_sem, out_send, out_recv, side_send, side_recv, back_send, back_recv, keep_sem):
    spread = ints * reps
    groups = pairs // 2
    me = lax.axis_index("pair")
    mine = lax.axis_index("int") * reps + lax.axis_index("rep")
    chip = me // 2
    rows = left.shape[1] * left.shape[2]
    width = slab.shape[1]
    chunks = slab_sem.shape[0]
    depth = slab.shape[0] // chunks

    def side(step):
        to = (mine + step) % spread
        return {"int": to // reps, "rep": to % reps}

    def load(i):
        part = pl.ds(i * depth, depth)
        return pltpu.make_async_copy(right.at[part], slab.at[part], slab_sem.at[i])

    def outward(j):
        to = flip(me, j, pairs)
        return pltpu.make_async_remote_copy(
            src_ref=packed.at[to], dst_ref=left.at[me, mine],
            send_sem=out_send.at[j], recv_sem=out_recv.at[j],
            device_id={"pair": to}, device_id_type=MESH)

    def arrived(j):
        came = flip(me, j, pairs)
        return pltpu.make_async_remote_copy(
            src_ref=packed.at[came], dst_ref=left.at[came, mine],
            send_sem=out_send.at[j], recv_sem=out_recv.at[j],
            device_id={"pair": came}, device_id_type=MESH)

    def sideways(j, step):
        at = flip(me, j, pairs)
        return pltpu.make_async_remote_copy(
            src_ref=left.at[at, mine], dst_ref=left.at[at, mine],
            send_sem=side_send.at[j, step - 1], recv_sem=side_recv.at[j, step - 1],
            device_id=side(step), device_id_type=MESH)

    def crossed(j, step):
        at = flip(me, j, pairs)
        came = (mine + spread - step) % spread
        return pltpu.make_async_remote_copy(
            src_ref=left.at[at, came], dst_ref=left.at[at, came],
            send_sem=side_send.at[j, step - 1], recv_sem=side_recv.at[j, step - 1],
            device_id=side(step), device_id_type=MESH)

    def back(j):
        to = flip(me, j, pairs)
        return pltpu.make_async_remote_copy(
            src_ref=product.at[to], dst_ref=returned.at[me],
            send_sem=back_send.at[j], recv_sem=back_recv.at[j],
            device_id={"pair": to}, device_id_type=MESH)

    def home(j):
        came = flip(me, j, pairs)
        return pltpu.make_async_remote_copy(
            src_ref=product.at[came], dst_ref=returned.at[came],
            send_sem=back_send.at[j], recv_sem=back_recv.at[j],
            device_id={"pair": came}, device_id_type=MESH)

    own = pltpu.make_async_copy(packed.at[me], left.at[me, mine], own_sem)
    keep = pltpu.make_async_copy(product.at[me], returned.at[me], keep_sem)

    own.start()
    barrier = pltpu.get_barrier_semaphore()
    for j in range(1, pairs):
        pl.semaphore_signal(barrier, inc=1, device_id={"pair": flip(me, j, pairs)}, device_id_type=MESH)
    for step in range(1, spread):
        pl.semaphore_signal(barrier, inc=1, device_id=side(step), device_id_type=MESH)
    pl.semaphore_wait(barrier, pairs + spread - 2)

    @pl.loop(0, pairs - 1)
    def _(i):
        outward(pairs - 1 - i).start()

    @pl.loop(0, chunks)
    def _(i):
        load(i).start()

    def multiply(group):
        at = flip(chip, group, groups)

        @pl.loop(0, width // tile)
        def _(t):
            cols = pl.ds(pl.multiple_of(t * tile, tile), tile)
            part = left[pl.ds(at * 2, 2)].reshape(2 * rows, left.shape[3])
            total = jnp.dot(part, slab[:, cols], preferred_element_type=jnp.float32)
            product[pl.ds(at * 2, 2), :, cols] = total.astype(jnp.bfloat16).reshape(2, rows, tile)

    own.wait()
    for step in range(1, spread):
        sideways(0, step).start()
    arrived(1).wait_recv()
    for step in range(1, spread):
        sideways(1, step).start()

    @pl.loop(0, chunks)
    def _(i):
        load(i).wait()

    for j in range(2):
        for step in range(1, spread):
            crossed(j, step).wait_recv()
    multiply(0)
    keep.start()
    back(1).start()

    @pl.loop(0, groups - 1)
    def _(i):
        group = groups - 1 - i
        for k in range(2):
            j = group * 2 + 1 - k
            arrived(j).wait_recv()
            for step in range(1, spread):
                sideways(j, step).start()
        for k in range(2):
            j = group * 2 + 1 - k
            for step in range(1, spread):
                crossed(j, step).wait_recv()
        multiply(group)
        for k in range(2):
            back(group * 2 + 1 - k).start()

    keep.wait()

    @pl.loop(0, pairs)
    def _(j):
        for step in range(1, spread):
            sideways(j, step).wait_send()

    @pl.loop(1, pairs)
    def _(j):
        outward(j).wait_send()
        back(j).wait_send()
        home(j).wait_recv()


def shards(ints, reps, amplitudes, amp_tiles, integrals, int_tiles, occupied_energy, virtual_energy):
    pairs = lax.axis_size("pair")
    spread = ints * reps
    tile_total = int_tiles.shape[0]
    row_tiles, slot_count, row_local, pair_width = amplitudes.shape
    couplings = integrals.shape[2]
    col_local = integrals.shape[3]
    width = couplings * col_local
    entries = row_tiles * slot_count
    capacity = max(2, (entries + tile_total - 1) // tile_total)
    flat_tiles = amp_tiles.reshape(-1)
    tile_hits = (flat_tiles[:, None] == jnp.arange(tile_total, dtype=jnp.int32)[None, :]).astype(
        jnp.int32
    )
    slot_rank = jnp.sum(tile_hits * (jnp.cumsum(tile_hits, axis=0) - 1), axis=1)
    slot_index = flat_tiles * capacity + slot_rank
    buffer_slots = tile_total * capacity
    dispatch = (jnp.arange(buffer_slots, dtype=jnp.int32)[:, None] == slot_index[None, :]).astype(
        jnp.bfloat16
    )
    right = integrals.reshape(pair_width, width)
    packed = jnp.dot(
        dispatch,
        amplitudes.reshape(entries, row_local * pair_width),
        preferred_element_type=jnp.float32,
    )
    held = capacity * row_local
    padded = -(-held // 16) * 16
    packed = packed.astype(jnp.bfloat16).reshape(pairs, held, pair_width)
    packed = jnp.pad(packed, ((0, 0), (0, padded - held), (0, 0)))
    rows = spread * padded
    chunks = 4
    dma = pltpu.SemaphoreType.DMA
    returned = pl.pallas_call(
        functools.partial(ladder, pairs, ints, reps, 512),
        out_shape=jax.ShapeDtypeStruct((pairs, rows, width), jnp.bfloat16),
        in_specs=[pl.BlockSpec(memory_space=pl.ANY)] * 2,
        out_specs=pl.BlockSpec(memory_space=pl.ANY),
        scratch_shapes=[
            pltpu.VMEM((pairs, spread, padded, pair_width), jnp.bfloat16),
            pltpu.VMEM((pair_width, width), jnp.bfloat16),
            pltpu.VMEM((pairs, rows, width), jnp.bfloat16),
            dma((chunks,)),
            dma,
            dma((pairs,)),
            dma((pairs,)),
            dma((pairs, spread - 1)),
            dma((pairs, spread - 1)),
            dma((pairs,)),
            dma((pairs,)),
            dma,
        ],
        compiler_params=pltpu.CompilerParams(
            collective_id=0, has_side_effects=True, vmem_limit_bytes=56 << 20
        ),
    )(packed, right)
    returned = returned.reshape(pairs, spread, padded, couplings, col_local)[:, :, :held]
    returned = returned.reshape(pairs, spread, capacity, row_local, couplings, col_local)
    targets = jnp.sum(tile_hits[:, :, None] * int_tiles[None, :, :], axis=1)
    row_owner = jnp.arange(entries, dtype=jnp.int32) // slot_count
    dest_rows = row_owner[:, None] * tile_total + targets
    landing = (
        jnp.arange(row_tiles * tile_total, dtype=jnp.int32)[:, None, None] == dest_rows[None, :, :]
    ).astype(jnp.bfloat16)
    combine = jnp.einsum(
        "qjk,sj->qsk", landing, dispatch, preferred_element_type=jnp.float32
    ).astype(jnp.bfloat16)
    combine = combine.reshape(row_tiles * tile_total, pairs, capacity, couplings)
    residual = jnp.einsum("qdak,dxalkc->qxlc", combine, returned, preferred_element_type=jnp.float32)
    residual = residual.reshape(row_tiles, tile_total, spread * row_local, col_local)
    denominator = virtual_energy[None, :, None, :] - occupied_energy[:, None, :, None]
    return (residual / denominator).astype(jnp.bfloat16)


def solution(mesh):
    placed = (
        P(("mol", "pair"), None, ("int", "rep"), None),
        P(("mol", "pair"), None),
        P(("mol", "pair"), None, None, ("int", "rep")),
        P("mol", None),
        P(("mol", "pair"), None),
        P("mol", ("int", "rep")),
    )
    return jax.shard_map(
        functools.partial(shards, mesh.shape["int"], mesh.shape["rep"]),
        mesh=mesh,
        in_specs=placed,
        out_specs=P(("mol", "pair"), None, None, ("int", "rep")),
        check_vma=False,
    )
```

time: 270 us -> 198 us (0.73)
  Pallas kernels: 0 us -> 142 us
  waiting for transfers between devices: 126 us -> 0 us
  blocking collectives: 55.3 us -> 0 us
  matrix products: 29.6 us -> 5.41 us
  between operations: 13.4 us -> 0.06 us
  local copies, waits for them, and re-layouts: 39.9 us -> 50.1 us
  starting transfers between devices: 4.86 us -> 0 us
    pallas_call x0 -> x1, Pallas kernels: none -> 142 us  [shards(): pl.pallas_call(functools.partial(ladder, pairs, ints, reps, 512), out_sha...]
    all_to_all x1 -> x0, waiting for transfers between devices: 93.5 us -> none  [shards(): lax.all_to_all(stacked, 'pair', split_axis=0, concat_axis=0, tiled=True)]
    all_to_all x1 -> x0, blocking collectives: 55.3 us -> none  [shards(): lax.all_to_all(packed, 'pair', split_axis=0, concat_axis=0, tiled=True)]
    all_gather x1 -> x0, waiting for transfers between devices: 32.2 us -> none  [shards(): lax.all_gather(lax.all_to_all(packed, 'pair', split_axis=0, concat_axis=0...]
    dot_general x2 -> x1, matrix products: 28.8 us -> 3.2 us  [shards(): jnp.einsum('qdak,dxalkc->qxlc', combine, returned, preferred_element_type...]
    dot_general x0 -> x2, local copies, waits for them, and re-layouts: none -> 8.69 us  [shards(): jnp.einsum('qdak,dxalkc->qxlc', combine, returned, preferred_element_type...]
    all_to_all x1 -> x0, starting transfers between devices: 4.86 us -> none  [shards(): lax.all_to_all(stacked, 'pair', split_axis=0, concat_axis=0, tiled=True)]
    reshape x0 -> x3, local copies, waits for them, and re-layouts: none -> 3.24 us  [the longest x1 3.15 us: shards(): packed = packed.astype(jnp.bfloat16).reshape(pairs, held, pair_width)]
  transfers between devices with their start and end apart: 2 -> 0, of which waited for: 2 -> 0; matrix products, arithmetic and copies ran while one was open for 9% -> 0% of each run, Pallas kernels for 0% -> 0%
where the time goes in v1:
time: 198 us
  Pallas kernels  142 us (72%)
  local copies, waits for them, and re-layouts  50.1 us (25%)
  matrix products  5.41 us (3%)
    pallas_call x1, Pallas kernels, shards(): pl.pallas_call(functools.partial(ladder, pairs, ints, reps, 512), out_sha...  142 us
    unnamed x10, local copies, waits for them, and re-layouts  26 us
    dot_general x2, local copies, waits for them, and re-layouts, shards(): jnp.einsum('qdak,dxalkc->qxlc', combine, returned, preferred_element_type...  8.69 us
    another operation x1, local copies, waits for them, and re-layouts, shards(): returned.reshape(pairs, spread, capacity, row_local, couplings, col_local)  7.8 us
    convert_element_type x1, local copies, waits for them, and re-layouts, shards(): return (residual / denominator).astype(jnp.bfloat16)  4.32 us

profile of v1, /device:TPU:0, one launch (start us, length us, event | category | flops | bytes accessed | tf_op | source)
XLA Modules:
  0.0 198.2 jit_solution(8251421468008032978)
XLA Ops:
  0.0 0.0 copy-start
  0.0 2.8 %copy.24 = bf16[2,8,16,4096]{3,1,2,0:T(8,128)(2,1)S(1)} copy(bf16[2,8,16,4096]{3,2,1,0:T(8,128)(2,1)} %bitcast.37) | data formatting | bytes 4194304
  2.8 0.0 copy-done
  2.8 0.1 reshape.84
  2.9 0.1 fusion.3
  3.0 0.2 select_reduce_fusion
  3.2 2.0 %convolution_convert_fusion = bf16[16,65536]{1,0:T(8,128)(2,1)} fusion(bf16[16,65536]{1,0:T(8,128)(2,1)S(1)} %bitcast.35, s32[16]{0:T(128)S(1)} %multiply_add_fusion), kind=kOutput, calls=%fused_computation | convolution fusion | flops 34603264 | bytes 4194368 | tf_op jit(solution)/shard_map/dot_general | solution.py:182
  5.2 3.1 %reshape.87.packed = bf16[8,32,4096]{2,1,0:T(8,128)(2,1)} reshape(bf16[16,65536]{1,0:T(8,128)(2,1)} %convolution_convert_fusion) | data formatting | bytes 4194304 | tf_op jit(solution)/shard_map/reshape | solution.py:189
  8.3 23.2 %copy.25 = bf16[512,8,2,2048]{3,1,2,0:T(8,128)(2,1)} copy(bf16[512,8,2,2048]{3,2,1,0:T(2,128)(2,1)} %bitcast.33) | data formatting | bytes 67108864
  31.5 142.2 %shard_map.64 = bf16[8,64,4096]{2,1,0:T(8,128)(2,1)} custom-call(bf16[8,32,4096]{2,1,0:T(8,128)(2,1)} %reshape.87.packed, bf16[4096,4096]{1,0:T(8,128)(2,1)} %bitcast.32), custom_call_target="tpu_custom_call" | custom-call | tf_op jit(solution)/shard_map/pallas_call | solution.py:194
  173.8 7.8 %reshape_reshape.3 = bf16[8,2,2,16,2,2048]{5,4,3,2,1,0:T(2,128)(2,1)} reshape(bf16[8,64,4096]{2,1,0:T(8,128)(2,1)} %shard_map.64) | data formatting | bytes 8388608 | tf_op jit(solution)/shard_map/reshape;reshape | solution.py:218
  181.6 0.0 copy-start.1
  181.6 0.0 copy-start.2
  181.6 0.0 copy-start.3
  181.6 8.6 %copy.17 = bf16[2,16,2048,2,8,2]{2,4,5,3,1,0:T(8,128)(2,1)} copy(bf16[2,16,2048,2,8,2]{2,5,1,3,0,4:T(2,128)(2,1)} %bitcast.34) | data formatting | bytes 8388608 | tf_op jit(solution)/shard_map/qdak,dxalkc->qxlc/dot_general | solution.py:229
  190.2 0.1 copy.15
  190.2 0.0 copy-done.1
  190.2 0.1 multiply_reduce_fusion
  190.3 0.2 convolution_convert_fusion.1
  190.5 0.1 dot_general.19
  190.6 0.0 copy-done.2
  190.6 0.0 copy-done.3
  190.6 3.2 %fusion = bf16[4,8,32,2048]{3,1,2,0:T(8,128)(2,1)S(1)} fusion(bf16[32,2048,2,8,2,1]{1,3,4,2,0,5:T(8,128)(2,1)} %bitcast.36, f32[4,32]{1,0:T(4,128)S(1)} %copy-done.3, f32[8,2048]{1,0:T(8,128)S(1)} %copy-done.2, bf16[4,8,2,8,2,1]{1,0,3,4,2,5:T(4,128)(2,1)S(1)} %bitcast.38), kind=kOutput, calls=%fused_computation.2 | convolution fusion | flops 140509184 | bytes 8456704 | tf_op jit(solution)/shard_map/qdak,dxalkc->qxlc/dot_general | solution.py:229
  193.9 4.3 %copy.19 = bf16[4,8,32,2048]{3,2,1,0:T(8,128)(2,1)} copy(bf16[4,8,32,2048]{3,1,2,0:T(8,128)(2,1)S(1)} %fusion) | data formatting | bytes 8388608 | tf_op jit(solution)/shard_map/convert_element_type | solution.py:232
  (5 shorter events, 0.1 us)
Async XLA Ops:
  0.0 2.8 %copy-start = (s32[4,4]{1,0:T(4,128)S(1)}, s32[4,4]{1,0:T(4,128)}, u32[]{:S(2)}) copy-start(s32[4,4]{1,0:T(4,128)} %param.7) | copy-start | bytes 196
  181.6 8.7 %copy-start.1 = (s32[8,2]{0,1:T(2,128)S(1)}, s32[8,2]{0,1:T(2,128)}, u32[]{:S(2)}) copy-start(s32[8,2]{0,1:T(2,128)} %param.9) | copy-start | bytes 196
  181.6 9.1 %copy-start.2 = (f32[8,2048]{1,0:T(8,128)S(1)}, f32[8,2048]{1,0:T(8,128)}, u32[]{:S(2)}) copy-start(f32[8,2048]{1,0:T(8,128)} %param.11) | copy-start | bytes 196612
  181.6 9.1 %copy-start.3 = (f32[4,32]{1,0:T(4,128)S(1)}, f32[4,32]{1,0:T(4,128)}, u32[]{:S(2)}) copy-start(f32[4,32]{1,0:T(4,128)} %param.10) | copy-start | bytes 1540

commit v2 on v1

--- a/solution.py
+++ b/solution.py
@@ -156,6 +156,37 @@
         outward(j).wait_send()
         back(j).wait_send()
         home(j).wait_recv()
+
+
+def pack(entries, capacity, tiles, ranks, amplitudes, packed, sem):
+    def move(j):
+        return pltpu.make_async_copy(
+            amplitudes.at[j], packed.at[tiles[j] * capacity + ranks[j]], sem.at[j]
+        )
+
+    for j in range(entries):
+        move(j).start()
+    for j in range(entries):
+        move(j).wait()
+
+
+def combine(row_tiles, slot_count, couplings, spread, row_local, tiles, ranks, targets, occupied, virtual, *refs):
+    parts, out, total = refs[:couplings], refs[couplings], refs[couplings + 1]
+    tile_total = out.shape[1]
+    total[...] = jnp.zeros_like(total)
+
+    for r in range(row_tiles):
+        for k in range(slot_count):
+            tile = tiles[r * slot_count + k]
+            rank = ranks[r * slot_count + k]
+            for m in range(couplings):
+                at = targets[tile * couplings + m]
+                for x in range(spread):
+                    span = pl.ds(x * row_local, row_local)
+                    total[r, at, span, :] += parts[m][tile, x, rank].astype(jnp.float32)
+        for b in range(tile_total):
+            denominator = virtual[b : b + 1, :] - occupied[r]
+            out[r, b] = (total[r, b] / denominator).astype(jnp.bfloat16)
 
 
 def shards(ints, reps, amplitudes, amp_tiles, integrals, int_tiles, occupied_energy, virtual_energy):
@@ -173,20 +204,17 @@
         jnp.int32
     )
     slot_rank = jnp.sum(tile_hits * (jnp.cumsum(tile_hits, axis=0) - 1), axis=1)
-    slot_index = flat_tiles * capacity + slot_rank
-    buffer_slots = tile_total * capacity
-    dispatch = (jnp.arange(buffer_slots, dtype=jnp.int32)[:, None] == slot_index[None, :]).astype(
-        jnp.bfloat16
-    )
     right = integrals.reshape(pair_width, width)
-    packed = jnp.dot(
-        dispatch,
-        amplitudes.reshape(entries, row_local * pair_width),
-        preferred_element_type=jnp.float32,
-    )
+    packed = pl.pallas_call(
+        functools.partial(pack, entries, capacity),
+        out_shape=jax.ShapeDtypeStruct((tile_total * capacity, row_local, pair_width), jnp.bfloat16),
+        in_specs=[pl.BlockSpec(memory_space=pltpu.SMEM)] * 2 + [pl.BlockSpec(memory_space=pl.ANY)],
+        out_specs=pl.BlockSpec(memory_space=pl.ANY),
+        scratch_shapes=[pltpu.SemaphoreType.DMA((entries,))],
+    )(flat_tiles, slot_rank, amplitudes.reshape(entries, row_local, pair_width))
     held = capacity * row_local
     padded = -(-held // 16) * 16
-    packed = packed.astype(jnp.bfloat16).reshape(pairs, held, pair_width)
+    packed = packed.reshape(pairs, held, pair_width)
     packed = jnp.pad(packed, ((0, 0), (0, padded - held), (0, 0)))
     rows = spread * padded
     chunks = 4
@@ -214,22 +242,36 @@
             collective_id=0, has_side_effects=True, vmem_limit_bytes=56 << 20
         ),
     )(packed, right)
-    returned = returned.reshape(pairs, spread, padded, couplings, col_local)[:, :, :held]
-    returned = returned.reshape(pairs, spread, capacity, row_local, couplings, col_local)
-    targets = jnp.sum(tile_hits[:, :, None] * int_tiles[None, :, :], axis=1)
-    row_owner = jnp.arange(entries, dtype=jnp.int32) // slot_count
-    dest_rows = row_owner[:, None] * tile_total + targets
-    landing = (
-        jnp.arange(row_tiles * tile_total, dtype=jnp.int32)[:, None, None] == dest_rows[None, :, :]
-    ).astype(jnp.bfloat16)
-    combine = jnp.einsum(
-        "qjk,sj->qsk", landing, dispatch, preferred_element_type=jnp.float32
-    ).astype(jnp.bfloat16)
-    combine = combine.reshape(row_tiles * tile_total, pairs, capacity, couplings)
-    residual = jnp.einsum("qdak,dxalkc->qxlc", combine, returned, preferred_element_type=jnp.float32)
-    residual = residual.reshape(row_tiles, tile_total, spread * row_local, col_local)
-    denominator = virtual_energy[None, :, None, :] - occupied_energy[:, None, :, None]
-    return (residual / denominator).astype(jnp.bfloat16)
+    returned = returned.reshape(pairs, spread, padded, width)[:, :, :held]
+    returned = returned.reshape(pairs, spread, capacity, row_local, width)
+    block = min(512, col_local)
+    steps = col_local // block
+    full_rows = spread * row_local
+
+    def columns(m):
+        return pl.BlockSpec(
+            (pairs, spread, capacity, row_local, block), lambda i, *_: (0, 0, 0, 0, m * steps + i)
+        )
+
+    return pl.pallas_call(
+        functools.partial(combine, row_tiles, slot_count, couplings, spread, row_local),
+        out_shape=jax.ShapeDtypeStruct((row_tiles, tile_total, full_rows, col_local), jnp.bfloat16),
+        grid_spec=pltpu.PrefetchScalarGridSpec(
+            num_scalar_prefetch=3,
+            grid=(steps,),
+            in_specs=[
+                pl.BlockSpec((row_tiles, full_rows, 1), lambda i, *_: (0, 0, 0)),
+                pl.BlockSpec((tile_total, block), lambda i, *_: (0, i)),
+            ]
+            + [columns(m) for m in range(couplings)],
+            out_specs=pl.BlockSpec(
+                (row_tiles, tile_total, full_rows, block), lambda i, *_: (0, 0, 0, i)
+            ),
+            scratch_shapes=[pltpu.VMEM((row_tiles, tile_total, full_rows, block), jnp.float32)],
+        ),
+        compiler_params=pltpu.CompilerParams(vmem_limit_bytes=32 << 20),
+    )(flat_tiles, slot_rank, int_tiles.reshape(-1), occupied_energy[:, :, None], virtual_energy,
+      *([returned] * couplings))
 
 
 def solution(mesh):

time: 198 us -> 240 us (1.21)
  Pallas kernels: 142 us -> 212 us
  local copies, waits for them, and re-layouts: 50.1 us -> 26.4 us
  matrix products: 5.41 us -> 0 us
    pallas_call x0 -> x2, Pallas kernels: none -> 70.1 us  [the longest x1 65.4 us: shards(): pl.pallas_call(functools.partial(pack, entries, capacity), out_shape=jax....]
    dot_general x2 -> x0, local copies, waits for them, and re-layouts: 8.69 us -> none  [shards(): jnp.einsum('qdak,dxalkc->qxlc', combine, returned, preferred_element_type...]
    another operation x1 -> x0, local copies, waits for them, and re-layouts: 7.8 us -> none  [shards(): returned.reshape(pairs, spread, capacity, row_local, couplings, col_local)]
    dot_general x3 -> x0, matrix products: 5.41 us -> none  [the longest x1 3.2 us: shards(): jnp.einsum('qdak,dxalkc->qxlc', combine, returned, preferred_element_type...]
    convert_element_type x2 -> x0, local copies, waits for them, and re-layouts: 4.38 us -> none  [the longest x1 4.32 us: shards(): return (residual / denominator).astype(jnp.bfloat16)]
    reshape x2 -> x1, local copies, waits for them, and re-layouts: 3.15 us -> 0.08 us  [shards(): int_tiles.reshape(-1)]
    unnamed x10 -> x16, local copies, waits for them, and re-layouts: 26 us -> 25.5 us
where the time goes in v2:
time: 240 us
  Pallas kernels  212 us (88%)
  local copies, waits for them, and re-layouts  26.4 us (11%)
    pallas_call x1, Pallas kernels, shards(): pl.pallas_call(functools.partial(ladder, pairs, ints, reps, 512), out_sha...  142 us
    pallas_call x1, Pallas kernels, shards(): pl.pallas_call(functools.partial(pack, entries, capacity), out_shape=jax....  65.4 us
    unnamed x16, local copies, waits for them, and re-layouts  25.5 us

profile of v2, /device:TPU:0, one launch (start us, length us, event | category | flops | bytes accessed | tf_op | source)
XLA Modules:
  0.0 239.8 jit_solution(3946152940675802079)
XLA Ops:
  0.0 0.8 reshape.16.tiles
  0.8 0.0 copy-start.2
  0.8 0.1 fusion
  0.9 0.7 select_reduce_fusion.ranks
  1.6 0.0 copy-done.2
  1.6 65.4 %shard_map.64 = bf16[16,16,4096]{2,1,0:T(8,128)(2,1)} custom-call(s32[16]{0:T(128)} %copy-done.2, s32[16]{0:T(128)} %select_reduce_fusion.ranks, bf16[16,16,4096]{2,1,0:T(8,128)(2,1)} %bitcast.12), custom_call_target="tpu_custom_call" | custom-call | tf_op jit(solution)/shard_map/pallas_call | solution.py:208
  67.0 23.2 %copy.11 = bf16[512,8,2,2048]{3,1,2,0:T(8,128)(2,1)} copy(bf16[512,8,2,2048]{3,2,1,0:T(2,128)(2,1)} %bitcast.10) | data formatting | bytes 67108864
  90.2 0.0 copy-start.5
  90.2 0.0 copy-start.6
  90.3 0.0 copy-start.1
  90.3 0.0 copy-start.3
  90.3 0.0 copy-start.4
  90.3 142.3 %shard_map.65 = bf16[8,64,4096]{2,1,0:T(8,128)(2,1)} custom-call(bf16[8,32,4096]{2,1,0:T(8,128)(2,1)} %bitcast.11, bf16[4096,4096]{1,0:T(8,128)(2,1)} %bitcast.9), custom_call_target="tpu_custom_call" | custom-call | tf_op jit(solution)/shard_map/pallas_call | solution.py:222
  232.6 0.0 copy-done.5
  232.6 0.1 copy.10.occupied
  232.7 0.0 copy-done.6
  232.7 0.1 copy.9
  232.8 0.1 reshape.17.targets
  232.9 0.0 copy-done.1
  232.9 0.0 copy-done.3
  232.9 0.0 copy-done.4
  232.9 0.0 copy-start
  232.9 2.2 copy-done
  235.1 4.7 %shard_map.66 = bf16[4,8,32,2048]{3,2,1,0:T(8,128)(2,1)} custom-call(s32[16]{0:T(128)S(1)} %copy-done.3, s32[16]{0:T(128)S(1)} %copy-done.4, s32[16]{0:T(128)S(1)} %reshape.17.targets, f32[4,32,1]{2,1,0:T(8,128)S(1)} %copy.10.occupied, f32[8,2048]{1,0:T(8,128)S(1)} %copy-done.1, bf16[8,2,2,16,4096]{4,3,2,1,0:T(8,128)(2,1)S(1)} %bitcast.7, ...), custom_call_target="tpu_custom_call" | custom-call | tf_op jit(solution)/shard_map/pallas_call | solution.py:256
  (1 shorter events, 0.0 us)
Async XLA Ops:
  0.8 0.8 copy-start.2
  90.2 142.4 %copy-start.5 = (f32[4,32]{1,0:T(4,128)S(1)}, f32[4,32]{1,0:T(4,128)}, u32[]{:S(2)}) copy-start(f32[4,32]{1,0:T(4,128)} %param.10) | copy-start | bytes 1540
  90.2 142.5 %copy-start.6 = (s32[8,2]{0,1:T(2,128)S(1)}, s32[8,2]{0,1:T(2,128)}, u32[]{:S(2)}) copy-start(s32[8,2]{0,1:T(2,128)} %param.9) | copy-start | bytes 196
  90.3 142.6 %copy-start.1 = (f32[8,2048]{1,0:T(8,128)S(1)}, f32[8,2048]{1,0:T(8,128)}, u32[]{:S(2)}) copy-start(f32[8,2048]{1,0:T(8,128)} %virtual.1) | copy-start | bytes 196612
  90.3 142.6 %copy-start.3 = (s32[16]{0:T(128)S(1)}, s32[16]{0:T(128)}, u32[]{:S(2)}) copy-start(s32[16]{0:T(128)} %copy-done.2) | copy-start | bytes 196
  90.3 142.6 %copy-start.4 = (s32[16]{0:T(128)S(1)}, s32[16]{0:T(128)}, u32[]{:S(2)}) copy-start(s32[16]{0:T(128)} %select_reduce_fusion.ranks) | copy-start | bytes 196
  232.9 2.2 copy-start

commit v3 on v2

--- a/solution.py
+++ b/solution.py
@@ -158,18 +158,6 @@
         home(j).wait_recv()
 
 
-def pack(entries, capacity, tiles, ranks, amplitudes, packed, sem):
-    def move(j):
-        return pltpu.make_async_copy(
-            amplitudes.at[j], packed.at[tiles[j] * capacity + ranks[j]], sem.at[j]
-        )
-
-    for j in range(entries):
-        move(j).start()
-    for j in range(entries):
-        move(j).wait()
-
-
 def combine(row_tiles, slot_count, couplings, spread, row_local, tiles, ranks, targets, occupied, virtual, *refs):
     parts, out, total = refs[:couplings], refs[couplings], refs[couplings + 1]
     tile_total = out.shape[1]
@@ -205,13 +193,16 @@
     )
     slot_rank = jnp.sum(tile_hits * (jnp.cumsum(tile_hits, axis=0) - 1), axis=1)
     right = integrals.reshape(pair_width, width)
-    packed = pl.pallas_call(
-        functools.partial(pack, entries, capacity),
-        out_shape=jax.ShapeDtypeStruct((tile_total * capacity, row_local, pair_width), jnp.bfloat16),
-        in_specs=[pl.BlockSpec(memory_space=pltpu.SMEM)] * 2 + [pl.BlockSpec(memory_space=pl.ANY)],
-        out_specs=pl.BlockSpec(memory_space=pl.ANY),
-        scratch_shapes=[pltpu.SemaphoreType.DMA((entries,))],
-    )(flat_tiles, slot_rank, amplitudes.reshape(entries, row_local, pair_width))
+    slot_index = flat_tiles * capacity + slot_rank
+    buffer_slots = tile_total * capacity
+    dispatch = (jnp.arange(buffer_slots, dtype=jnp.int32)[:, None] == slot_index[None, :]).astype(
+        jnp.bfloat16
+    )
+    packed = jnp.dot(
+        dispatch,
+        amplitudes.reshape(entries, row_local * pair_width),
+        preferred_element_type=jnp.float32,
+    ).astype(jnp.bfloat16)
     held = capacity * row_local
     padded = -(-held // 16) * 16
     packed = packed.reshape(pairs, held, pair_width)

time: 240 us -> 179 us (0.75)
  Pallas kernels: 212 us -> 147 us
  local copies, waits for them, and re-layouts: 26.4 us -> 31.1 us
    pallas_call x1 -> x0, Pallas kernels: 65.4 us -> none  [shards(): pl.pallas_call(functools.partial(pack, entries, capacity), out_shape=jax....]
    unnamed x16 -> x11, local copies, waits for them, and re-layouts: 25.5 us -> 28.2 us
where the time goes in v3:
time: 179 us
  Pallas kernels  147 us (82%)
  local copies, waits for them, and re-layouts  31.1 us (17%)
    pallas_call x1, Pallas kernels, shards(): pl.pallas_call(functools.partial(ladder, pairs, ints, reps, 512), out_sha...  142 us
    unnamed x11, local copies, waits for them, and re-layouts  28.2 us
    pallas_call x1, Pallas kernels, shards(): pl.pallas_call(functools.partial(combine, row_tiles, slot_count, coupling...  4.78 us

profile of v3, /device:TPU:0, one launch (start us, length us, event | category | flops | bytes accessed | tf_op | source)
XLA Modules:
  0.0 179.3 jit_solution(10398906173727015712)
XLA Ops:
  0.0 0.8 reshape.24.tiles
  0.8 0.1 fusion
  0.9 0.2 select_reduce_fusion.ranks
  1.1 2.7 %copy.11 = bf16[2,8,16,4096]{3,1,2,0:T(8,128)(2,1)S(1)} copy(bf16[2,8,16,4096]{3,2,1,0:T(8,128)(2,1)} %bitcast.14) | data formatting | bytes 4194304
  3.8 0.7 convolution_convert_fusion
  4.5 2.0 %reshape.27.packed = bf16[8,32,4096]{2,1,0:T(8,128)(2,1)} reshape(bf16[16,65536]{1,0:T(8,128)(2,1)S(1)} %convolution_convert_fusion) | data formatting | bytes 4194304 | tf_op jit(solution)/shard_map/reshape | solution.py:208
  6.5 23.2 %copy.12 = bf16[512,8,2,2048]{3,1,2,0:T(8,128)(2,1)} copy(bf16[512,8,2,2048]{3,2,1,0:T(2,128)(2,1)} %bitcast.12) | data formatting | bytes 67108864
  29.7 0.0 copy-start.2
  29.7 0.0 copy-start.3
  29.7 0.0 copy-start.1
  29.7 142.3 %shard_map.64 = bf16[8,64,4096]{2,1,0:T(8,128)(2,1)} custom-call(bf16[8,32,4096]{2,1,0:T(8,128)(2,1)} %reshape.27.packed, bf16[4096,4096]{1,0:T(8,128)(2,1)} %bitcast.11), custom_call_target="tpu_custom_call" | custom-call | tf_op jit(solution)/shard_map/pallas_call | solution.py:213
  172.0 0.0 copy-done.2
  172.0 0.1 copy.10.occupied
  172.1 0.0 copy-done.3
  172.1 0.1 copy.9
  172.2 0.1 reshape.25.targets
  172.3 0.0 copy-done.1
  172.3 0.0 copy-start
  172.3 2.2 %copy-done = bf16[8,64,4096]{2,1,0:T(8,128)(2,1)S(1)} copy-done((bf16[8,64,4096]{2,1,0:T(8,128)(2,1)S(1)}, bf16[8,64,4096]{2,1,0:T(8,128)(2,1)}, u32[]{:S(2)}) %copy-start) | copy-done | bytes 4194328
  174.5 4.8 %shard_map.65 = bf16[4,8,32,2048]{3,2,1,0:T(8,128)(2,1)} custom-call(s32[16]{0:T(128)S(1)} %reshape.24.tiles, s32[16]{0:T(128)S(1)} %select_reduce_fusion.ranks, s32[16]{0:T(128)S(1)} %reshape.25.targets, f32[4,32,1]{2,1,0:T(8,128)S(1)} %copy.10.occupied, f32[8,2048]{1,0:T(8,128)S(1)} %copy-done.1, bf16[8,2,2,16,4096]{4,3,2,1,0:T(8,128)(2,1)S(1)} %bitcast.9, ...), custom_call_target="tpu_custom_call" | custom-call | tf_op jit(solution)/shard_map/pallas_call | solution.py:247
  (2 shorter events, 0.0 us)
Async XLA Ops:
  29.7 142.3 %copy-start.2 = (f32[4,32]{1,0:T(4,128)S(1)}, f32[4,32]{1,0:T(4,128)}, u32[]{:S(2)}) copy-start(f32[4,32]{1,0:T(4,128)} %param.10) | copy-start | bytes 1540
  29.7 142.5 %copy-start.3 = (s32[8,2]{0,1:T(2,128)S(1)}, s32[8,2]{0,1:T(2,128)}, u32[]{:S(2)}) copy-start(s32[8,2]{0,1:T(2,128)} %param.9) | copy-start | bytes 196
  29.7 142.6 %copy-start.1 = (f32[8,2048]{1,0:T(8,128)S(1)}, f32[8,2048]{1,0:T(8,128)}, u32[]{:S(2)}) copy-start(f32[8,2048]{1,0:T(8,128)} %virtual.1) | copy-start | bytes 196612
  172.3 2.2 %copy-start = (bf16[8,64,4096]{2,1,0:T(8,128)(2,1)S(1)}, bf16[8,64,4096]{2,1,0:T(8,128)(2,1)}, u32[]{:S(2)}) copy-start(bf16[8,64,4096]{2,1,0:T(8,128)(2,1)} %shard_map.64) | copy-start | bytes 12582916
